TPU v7x, 32 devices: a whole 2x2x4 slice. The times are simulated.
32 devices in a mesh: row: 4 (over y, core), col: 2 (over x), rep: 4 (over z).
Axes of the slice: x: 2, y: 2, z: 4, core: 2. Of those that a mesh axis runs over, the one named last changes fastest.
Arguments:
- a_weights: bfloat16 [4, 4096, 512], P('rep', 'row', 'col'), may hold values from 0 to 10000, as said below
- a_flags: int32 [4, 32, 4], P('rep', 'row', 'col'), may hold values 0 or 1
- b_weights: bfloat16 [4, 512, 4096], P('rep', 'row', 'col'), may hold values from 0 to 10000, as said below
- b_flags: int32 [4, 4, 32], P('rep', 'row', 'col'), may hold values 0 or 1
- out_flags: int32 [32, 32], P('row', ('col', 'rep')), may hold values 0 or 1
Outputs:
- two_hop: bfloat16 [4096, 4096], P('row', ('col', 'rep'))
Inputs may be any that keep to these rules, and one draw needn't show every extreme that they name: `a_weights`: positive edge weights. `b_weights`: positive edge weights.
All inputs are finite; a program needn't handle non-finite values. No bound on the sum of `a_flags` or of `b_flags` or of `out_flags` on one device may be relied on, other than what follows from the above.
Results may differ from a plain program's by a relative error of at most 0.012.
Values may be sent and summed in bfloat16 or wider, within the bound.
A program may use at most 64 MiB of HBM per device.

v0:
```python
import jax
import jax.numpy as jnp
from jax import lax
from jax.sharding import PartitionSpec as P


def expand(flags, width):
    return jnp.repeat(jnp.repeat(flags, width, axis=-2), width, axis=-1)


def shards(a_weights, a_flags, b_weights, b_flags, out_flags):
    width = a_weights.shape[1] // a_flags.shape[1]
    a_masked = a_weights * expand(a_flags, width).astype(jnp.bfloat16)
    b_masked = b_weights * expand(b_flags, width).astype(jnp.bfloat16)
    deg_a = 1.0 + lax.psum(jnp.sum(a_masked, axis=(0, 2), dtype=jnp.float32), ("col", "rep"))
    walk_local = (a_masked.astype(jnp.float32) / deg_a[None, :, None]).astype(jnp.bfloat16)
    walk_a = lax.all_gather(walk_local, "col", axis=2, tiled=True)
    deg_b = 1.0 + lax.psum(jnp.sum(b_masked, axis=2, dtype=jnp.float32), "col")
    walk_b = (b_masked.astype(jnp.float32) / deg_b[:, :, None]).astype(jnp.bfloat16)
    left_rows = walk_a[0]
    partial_sum = jnp.dot(
        left_rows,
        lax.all_gather(walk_b, "row", axis=1, tiled=True)[0],
        preferred_element_type=jnp.float32,
    )
    summed = lax.psum_scatter(
        partial_sum.astype(jnp.bfloat16), "rep", scatter_dimension=1, tiled=True
    ).astype(jnp.float32)
    factor = jnp.float32(b_weights.shape[2] * lax.axis_size("col"))
    return (factor * summed * expand(out_flags, width).astype(jnp.float32)).astype(jnp.bfloat16)


def solution(mesh):
    return jax.shard_map(
        shards,
        mesh=mesh,
        in_specs=(
            P("rep", "row", "col"),
            P("rep", "row", "col"),
            P("rep", "row", "col"),
            P("rep", "row", "col"),
            P("row", ("col", "rep")),
        ),
        out_specs=P("row", ("col", "rep")),
        check_vma=False,
    )
```

profile of v0, /device:TPU:1, one launch (start us, length us, event | category | flops | bytes accessed | tf_op | source)
XLA Modules:
  0.0 169.9 jit_solution(3243005505417846426)
XLA Ops:
  6.5 0.0 copy-start
  6.5 0.0 all-gather.3.cloned.1.call-start
  6.5 0.7 convert_bitcast_fusion.1
  7.3 0.1 copy.6
  7.4 2.9 %broadcast_in_dim.21 = bf16[1024,2,128]{2,1,0:T(2,128)(2,1)S(1)} broadcast(bf16[1024,2]{1,0:T(8,128)(2,1)S(1)} %bitcast.24), dimensions={0,1} | broadcast | bytes 528384 | tf_op jit(solution)/shard_map/broadcast_in_dim | solution.py:8
  10.4 0.0 copy-start.4
  10.4 0.0 copy-start.1
  10.4 0.3 convert_element_type.72
  10.7 0.0 copy-done
  10.7 0.2 convert_reduce_fusion.1
  11.0 18.8 %psum.14 = f32[1024]{0:T(1024)S(1)} all-reduce(f32[1024]{0:T(1024)S(1)} %convert_reduce_fusion.1), channel_id=1, replica_groups=mesh['row'=4,'col'=2,'rep'=4] {'col','rep'}, use_global_device_ids=true, to_apply=%region_1.0 | all-reduce | flops 1024 | bytes 8192 | tf_op jit(solution)/shard_map/psum | solution.py:15
  29.8 1.0 fusion.2
  30.8 0.0 all-gather.3.cloned.1.call-update
  30.8 0.0 all-gather.5.cloned.1.call-start
  30.9 0.0 copy-done.4
  30.9 0.1 broadcast_bitcast_fusion
  31.0 0.0 copy-done.1
  31.0 0.2 convert_reduce_fusion
  31.1 3.8 %psum.15 = f32[1,128]{1,0:T(1,128)S(1)} all-reduce(f32[1,128]{1,0:T(1,128)S(1)} %bitcast.25), channel_id=1, replica_groups=mesh['row'=4,'col'=2,'rep'=4] {'col'}, use_global_device_ids=true, to_apply=%region_3.0 | all-reduce | flops 128 | bytes 1024 | tf_op jit(solution)/shard_map/psum | solution.py:18
  34.9 1.0 fusion.3
  35.9 0.0 all-gather.5.cloned.1.call-update
  35.9 0.0 reduce-scatter.2.cloned.1.call-start
  36.0 17.4 %all-gather.3.cloned.1.call-done = bf16[1,1024,512]{2,1,0:T(8,128)(2,1)} async-done(((bf16[1,1024,256]{2,1,0:T(8,128)(2,1)}), bf16[1,1024,512]{2,1,0:T(8,128)(2,1)}) %all-gather.3.cloned.1.call-update) | async-done | bytes 1048592 | tf_op jit(solution)/shard_map/all_gather | solution.py:17
  53.4 24.6 %all-gather.5.cloned.1.call-done = bf16[1,512,2048]{2,1,0:T(8,128)(2,1)} async-done(((bf16[1,128,2048]{2,1,0:T(8,128)(2,1)}), bf16[1,512,2048]{2,1,0:T(8,128)(2,1)}) %all-gather.5.cloned.1.call-update) | async-done | bytes 2097168 | tf_op jit(solution)/shard_map/all_gather | solution.py:23
  77.9 6.2 %convolution_convert_fusion = bf16[1024,2048]{1,0:T(8,128)(2,1)} fusion(bf16[1,512,2048]{2,1,0:T(8,128)(2,1)} %all-gather.5.cloned.1.call-done, bf16[1,1024,512]{2,1,0:T(8,128)(2,1)} %all-gather.3.cloned.1.call-done), kind=kOutput, calls=%fused_computation | convolution fusion | flops 2149580800 | bytes 7340032 | tf_op jit(solution)/shard_map/dot_general | solution.py:21
  84.1 0.0 copy-start.3
  84.1 0.0 reduce-scatter.2.cloned.1.call-update
  84.2 0.7 copy-done.3
  84.8 0.1 copy.7
  84.9 75.8 %reduce-scatter.2.cloned.1.call-done = bf16[1024,512]{1,0:T(8,128)(2,1)} async-done(((bf16[1024,2048]{1,0:T(8,128)(2,1)}), bf16[1024,512]{1,0:T(8,128)(2,1)}) %reduce-scatter.2.cloned.1.call-update) | async-done | bytes 1048592 | tf_op jit(solution)/shard_map/reduce_scatter | solution.py:26
  160.7 0.0 copy-start.2
  160.8 1.2 broadcast_in_dim.25
  162.0 0.0 copy-done.2
  162.0 1.4 fusion
  (6 shorter events, 0.1 us)
Async XLA Ops:
  6.5 4.2 %copy-start = (bf16[1,1024,256]{2,1,0:T(8,128)(2,1)S(1)}, bf16[1,1024,256]{2,1,0:T(8,128)(2,1)}, u32[]{:S(2)}) copy-start(bf16[1,1024,256]{2,1,0:T(8,128)(2,1)} %param.5) | copy-start | bytes 1572868
  6.5 46.8 %all-gather.3.cloned.1.call-start = ((), (), s32[]{:S(2)}) async-start(), calls=%async_computation.1 | async-start | bytes 1572864 | tf_op jit(solution)/shard_map/all_gather | solution.py:17
  10.4 20.5 %copy-start.4 = (s32[1,1,16]{2,1,0:T(1,128)S(1)}, s32[1,1,16]{2,1,0:T(1,128)}, u32[]{:S(2)}) copy-start(s32[1,1,16]{2,1,0:T(1,128)} %param.8) | copy-start | bytes 196
  10.4 20.6 %copy-start.1 = (bf16[1,128,2048]{2,1,0:T(8,128)(2,1)S(1)}, bf16[1,128,2048]{2,1,0:T(8,128)(2,1)}, u32[]{:S(2)}) copy-start(bf16[1,128,2048]{2,1,0:T(8,128)(2,1)} %param.7) | copy-start | bytes 1572868
  30.8 47.1 %all-gather.5.cloned.1.call-start = ((), (), s32[]{:S(2)}) async-start(), calls=%async_computation.2 | async-start | bytes 2621440 | tf_op jit(solution)/shard_map/all_gather | solution.py:23
  35.9 124.8 %reduce-scatter.2.cloned.1.call-start = ((), (), s32[]{:S(2)}) async-start(), calls=%async_computation.3 | async-start | bytes 5242880 | tf_op jit(solution)/shard_map/reduce_scatter | solution.py:26
  84.1 0.7 copy-start.3
  160.7 1.3 copy-start.2
Sparse Core Ops, SparseCore 0:
  30.9 22.3 all-gather.2
  54.9 22.9 all-gather.4
  84.3 76.3 reduce-scatter.1
where the time goes:
time: 171 us; the launch traced here: 170 us
  waiting for transfers between devices  118 us (69%)
  blocking collectives  22.6 us (13%)
  between operations  13.2 us (8%)
  matrix products  6.19 us (4%)
  local copies, waits for them, and re-layouts  5.51 us (3%)
  other arithmetic  4.51 us (3%)
    reduce_scatter x1, waiting for transfers between devices, shards(): lax.psum_scatter(partial_sum.astype(jnp.bfloat16), 'rep', scatter_dimensi...  75.8 us
    all_gather x1, waiting for transfers between devices, shards(): lax.all_gather(walk_b, 'row', axis=1, tiled=True)[0]  24.6 us
    psum x1, blocking collectives, shards(): lax.psum(jnp.sum(a_masked, axis=(0, 2), dtype=jnp.float32), ('col', 'rep'))  18.8 us
    all_gather x1, waiting for transfers between devices, shards(): walk_a = lax.all_gather(walk_local, 'col', axis=2, tiled=True)  17.4 us
    dot_general x1, matrix products, shards(): jnp.dot(left_rows, lax.all_gather(walk_b, 'row', axis=1, tiled=True)[0],...  6.19 us
    broadcast_in_dim x4, local copies, waits for them, and re-layouts, expand(): return jnp.repeat(jnp.repeat(flags, width, axis=-2), width, axis=-1)  4.25 us
    psum x1, blocking collectives, shards(): deg_b = 1.0 + lax.psum(jnp.sum(b_masked, axis=2, dtype=jnp.float32), 'col')  3.79 us
  transfers between devices with their start and end apart: 3, of which 3 were waited for; matrix products, arithmetic and copies ran while one was open for 1% of the time, Pallas kernels for 0%

commit v1 on v0

v1 whole, which is shorter than its diff:
```python
import functools

import jax
import jax.numpy as jnp
from jax import lax
from jax.experimental import pallas as pl
from jax.experimental.pallas import tpu as pltpu
from jax.sharding import PartitionSpec as P

MESH = pl.DeviceIdType.MESH


def kernel(
    n_r, n_c, n_p, nch, factor,
    af, bf, of, a, b, out,
    abuf, bm, bsl, bbuf, dego, degr, acc, dacc,
    zr, zsl, zsr, xr, xs, bzr, bzs, byr, bys, dr, ds,
):
    r, c, p = lax.axis_index("row"), lax.axis_index("col"), lax.axis_index("rep")
    rows, ka = a.shape
    kb = b.shape[0]
    width = rows // af.shape[0]
    cols = out.shape[1]
    ch_rows = rows // nch

    barrier = pltpu.get_barrier_semaphore()
    for axis, mine, count in (("row", r, n_r), ("col", c, n_c), ("rep", p, n_p)):
        for o in range(1, count):
            pl.semaphore_signal(
                barrier, inc=1, device_id={axis: lax.rem(mine + o, count)}, device_id_type=MESH
            )

    for i in range(bf.shape[0]):
        for j in range(bf.shape[1]):
            at = (slice(i * width, (i + 1) * width), slice(j * width, (j + 1) * width))
            bm[at] = (b[at].astype(jnp.float32) * bf[i, j].astype(jnp.float32)).astype(jnp.bfloat16)
    dego[...] = jnp.dot(
        bm[...], jnp.ones((bm.shape[1], 128), jnp.bfloat16), preferred_element_type=jnp.float32
    )
    for i in range(af.shape[0]):
        ch, off = divmod(i * width, ch_rows)
        for j in range(af.shape[1]):
            tile = a[i * width:(i + 1) * width, j * width:(j + 1) * width].astype(jnp.float32)
            abuf[p, c, ch, off:off + width, j * width:(j + 1) * width] = (
                tile * af[i, j].astype(jnp.float32)
            ).astype(jnp.bfloat16)

    pl.semaphore_wait(barrier, n_r + n_c + n_p - 3)

    def deg_copy(cc):
        return pltpu.make_async_remote_copy(
            src_ref=dego, dst_ref=degr.at[c], send_sem=ds.at[cc], recv_sem=dr.at[c],
            device_id={"col": cc}, device_id_type=MESH)

    def z_copy(g, ch, to, send):
        block = abuf.at[g, c, ch]
        return pltpu.make_async_remote_copy(
            src_ref=block, dst_ref=block, send_sem=send.at[g, ch], recv_sem=zr.at[g, ch],
            device_id={"rep": to}, device_id_type=MESH)

    def x_copy(g, ch, cc):
        block = abuf.at[g, c, ch]
        return pltpu.make_async_remote_copy(
            src_ref=block, dst_ref=block, send_sem=xs.at[g, cc, ch], recv_sem=xr.at[g, c, ch],
            device_id={"col": cc}, device_id_type=MESH)

    def bz_copy(pp):
        return pltpu.make_async_remote_copy(
            src_ref=bsl.at[pp], dst_ref=bbuf.at[p, pl.ds(pl.multiple_of(r * kb, kb), kb)],
            send_sem=bzs.at[pp], recv_sem=bzr.at[p], device_id={"rep": pp}, device_id_type=MESH)

    def by_copy(g, rr):
        block = bbuf.at[g, pl.ds(pl.multiple_of(r * kb, kb), kb)]
        return pltpu.make_async_remote_copy(
            src_ref=block, dst_ref=block, send_sem=bys.at[g, rr], recv_sem=byr.at[g, r],
            device_id={"row": rr}, device_id_type=MESH)

    def arrived(ref, sem):
        pltpu.make_async_copy(ref, ref, sem).wait()

    def others(mine, count, f):
        @pl.loop(1, count)
        def _(o):
            f(lax.rem(mine + o, count))

    def forward(g, ch):
        others(c, n_c, lambda cc: x_copy(g, ch, cc).start())

    others(c, n_c, lambda cc: deg_copy(cc).start())

    @pl.loop(0, nch)
    def _(ch):
        @pl.when(p > 0)
        def _():
            z_copy(p, ch, p - 1, zsl).start()

        @pl.when(p < n_p - 1)
        def _():
            z_copy(p, ch, p + 1, zsr).start()

        forward(p, ch)

    def add_deg(cc):
        arrived(degr.at[cc], dr.at[cc])
        dego_sum[...] += degr[cc]

    dego_sum = dacc.at[pl.ds(0, kb)]
    dego_sum[...] = 1.0 + dego[...]
    others(c, n_c, add_deg)
    for t in range(bm.shape[1] // 128):
        pp, off = divmod(t * 128, cols)
        bsl[pp, :, off:off + 128] = (
            bm[:, t * 128:(t + 1) * 128].astype(jnp.float32) / dego_sum[...]
        ).astype(jnp.bfloat16)
    others(p, n_p, lambda pp: bz_copy(pp).start())
    bbuf[p, pl.ds(pl.multiple_of(r * kb, kb), kb)] = bsl[p]
    others(r, n_r, lambda rr: by_copy(p, rr).start())

    for d in range(1, n_p):
        @pl.loop(0, nch)
        def _(ch):
            @pl.when(p >= d)
            def _():
                g = p - d
                arrived(abuf.at[g, c, ch], zr.at[g, ch])

                @pl.when(p < n_p - 1)
                def _():
                    z_copy(g, ch, p + 1, zsr).start()

                forward(g, ch)

            @pl.when(p + d < n_p)
            def _():
                g = p + d
                arrived(abuf.at[g, c, ch], zr.at[g, ch])

                @pl.when(p > 0)
                def _():
                    z_copy(g, ch, p - 1, zsl).start()

                forward(g, ch)

        def pass_b(g):
            arrived(bbuf.at[g, pl.ds(pl.multiple_of(r * kb, kb), kb)], bzr.at[g])
            others(r, n_r, lambda rr: by_copy(g, rr).start())

        @pl.when(p >= d)
        def _():
            pass_b(p - d)

        @pl.when(p + d < n_p)
        def _():
            pass_b(p + d)

    acc[...] = jnp.zeros_like(acc)
    dacc[...] = jnp.ones_like(dacc)

    def block(g, cc, ch):
        left = abuf[g, cc, ch]
        right = bbuf[g, pl.ds(pl.multiple_of(cc * ka, ka), ka)]
        at = pl.ds(pl.multiple_of(ch * ch_rows, ch_rows), ch_rows)
        acc[at] += jnp.dot(left, right, preferred_element_type=jnp.float32)
        dacc[at] += jnp.dot(
            left, jnp.ones((ka, 128), jnp.bfloat16), preferred_element_type=jnp.float32
        )

    def by_side(f):
        for d in range(n_p):
            @pl.when(p >= d)
            def _():
                f(p - d)

            if d:
                @pl.when(p + d < n_p)
                def _():
                    f(p + d)

    def own(g):
        def wait_b(rr):
            arrived(bbuf.at[g, pl.ds(pl.multiple_of(rr * kb, kb), kb)], byr.at[g, rr])

        others(r, n_r, wait_b)

        @pl.loop(0, nch)
        def _(ch):
            block(g, c, ch)

    by_side(own)

    def crossed(g):
        def one(cc):
            @pl.loop(0, nch)
            def _(ch):
                arrived(abuf.at[g, cc, ch], xr.at[g, cc, ch])
                block(g, cc, ch)

        others(c, n_c, one)

    by_side(crossed)

    @pl.loop(0, of.shape[0])
    def _(i):
        at = pl.ds(pl.multiple_of(i * width, width), width)
        scale = factor / dacc[at]
        for j in range(of.shape[1]):
            tile = slice(j * width, (j + 1) * width)
            out[at, tile] = (
                acc[at, tile] * (scale * of[i, j].astype(jnp.float32))
            ).astype(jnp.bfloat16)

    others(c, n_c, lambda cc: deg_copy(cc).wait_send())
    others(p, n_p, lambda pp: bz_copy(pp).wait_send())

    @pl.loop(0, n_p)
    def _(g):
        others(r, n_r, lambda rr: by_copy(g, rr).wait_send())

        @pl.loop(0, nch)
        def _(ch):
            others(c, n_c, lambda cc: x_copy(g, ch, cc).wait_send())

            @pl.when((g >= p) & (p > 0))
            def _():
                z_copy(g, ch, p - 1, zsl).wait_send()

            @pl.when((g <= p) & (p < n_p - 1))
            def _():
                z_copy(g, ch, p + 1, zsr).wait_send()


def shards(a_weights, a_flags, b_weights, b_flags, out_flags):
    n_r, n_c, n_p = (lax.axis_size(axis) for axis in ("row", "col", "rep"))
    _, rows, ka = a_weights.shape
    _, kb, wide = b_weights.shape
    cols = wide // n_p
    nch = max(1, 8 // n_c)
    dma = pltpu.SemaphoreType.DMA
    smem = pl.BlockSpec(memory_space=pltpu.SMEM)
    vmem = pl.BlockSpec(memory_space=pltpu.VMEM)
    return pl.pallas_call(
        functools.partial(kernel, n_r, n_c, n_p, nch, float(wide * n_c)),
        out_shape=jax.ShapeDtypeStruct((rows, cols), jnp.bfloat16),
        in_specs=[smem] * 3 + [vmem] * 2,
        out_specs=vmem,
        scratch_shapes=[
            pltpu.VMEM((n_p, n_c, nch, rows // nch, ka), jnp.bfloat16),
            pltpu.VMEM((kb, wide), jnp.bfloat16),
            pltpu.VMEM((n_p, kb, cols), jnp.bfloat16),
            pltpu.VMEM((n_p, n_r * kb, cols), jnp.bfloat16),
            pltpu.VMEM((kb, 128), jnp.float32),
            pltpu.VMEM((n_c, kb, 128), jnp.float32),
            pltpu.VMEM((rows, cols), jnp.float32),
            pltpu.VMEM((rows, 128), jnp.float32),
            dma((n_p, nch)), dma((n_p, nch)), dma((n_p, nch)),
            dma((n_p, n_c, nch)), dma((n_p, n_c, nch)),
            dma((n_p,)), dma((n_p,)),
            dma((n_p, n_r)), dma((n_p, n_r)),
            dma((n_c,)), dma((n_c,)),
        ],
        compiler_params=pltpu.CompilerParams(
            collective_id=0, has_side_effects=True, vmem_limit_bytes=56 * 2**20
        ),
    )(a_flags[0], b_flags[0], out_flags, a_weights[0], b_weights[0])


def solution(mesh):
    return jax.shard_map(
        shards,
        mesh=mesh,
        in_specs=(
            P("rep", "row", "col"),
            P("rep", "row", "col"),
            P("rep", "row", "col"),
            P("rep", "row", "col"),
            P("row", ("col", "rep")),
        ),
        out_specs=P("row", ("col", "rep")),
        check_vma=False,
    )
```

time: 171 us -> 68.9 us (0.40)
  waiting for transfers between devices: 118 us -> 0 us
  Pallas kernels: 0 us -> 64.4 us
  blocking collectives: 22.6 us -> 0 us
  between operations: 13.2 us -> 0.01 us
  matrix products: 6.19 us -> 0 us
  other arithmetic: 4.51 us -> 0 us
    reduce_scatter x1 -> x0, waiting for transfers between devices: 75.8 us -> none  [shards(): lax.psum_scatter(partial_sum.astype(jnp.bfloat16), 'rep', scatter_dimensi...]
    pallas_call x0 -> x1, Pallas kernels: none -> 64.4 us  [shards(): pl.pallas_call(functools.partial(kernel, n_r, n_c, n_p, nch, float(wide *...]
    all_gather x2 -> x0, waiting for transfers between devices: 42 us -> none  [the longest x1 24.6 us: shards(): lax.all_gather(walk_b, 'row', axis=1, tiled=True)[0]]
    psum x2 -> x0, blocking collectives: 22.6 us -> none  [the longest x1 18.8 us: shards(): lax.psum(jnp.sum(a_masked, axis=(0, 2), dtype=jnp.float32), ('col', 'rep'))]
    dot_general x1 -> x0, matrix products: 6.19 us -> none  [shards(): jnp.dot(left_rows, lax.all_gather(walk_b, 'row', axis=1, tiled=True)[0],...]
    broadcast_in_dim x4 -> x0, local copies, waits for them, and re-layouts: 4.25 us -> none  [expand(): return jnp.repeat(jnp.repeat(flags, width, axis=-2), width, axis=-1)]
    convert_element_type x6 -> x0, other arithmetic: 4.09 us -> none  [the longest x1 1.39 us: shards(): (factor * summed * expand(out_flags, width).astype(jnp.float32)).astype(j...]
    unnamed x10 -> x6, local copies, waits for them, and re-layouts: 0.68 us -> 3.62 us
  transfers between devices with their start and end apart: 3 -> 0, of which waited for: 3 -> 0; matrix products, arithmetic and copies ran while one was open for 1% -> 0% of each run, Pallas kernels for 0% -> 0%
where the time goes in v1:
time: 68.9 us; the launch traced here: 68.7 us
  Pallas kernels  64.4 us (93%)
  local copies, waits for them, and re-layouts  4.29 us (6%)
    pallas_call x1, Pallas kernels, shards(): pl.pallas_call(functools.partial(kernel, n_r, n_c, n_p, nch, float(wide *...  64.4 us
    unnamed x6, local copies, waits for them, and re-layouts  3.62 us

profile of v1, /device:TPU:1, one launch (start us, length us, event | category | flops | bytes accessed | tf_op | source)
XLA Modules:
  0.0 68.7 jit_solution(17638655109930062049)
XLA Ops:
  0.0 0.0 copy-start.1
  0.0 0.7 copy-done.1
  0.7 0.0 copy-start
  0.7 0.7 copy.6.af
  1.4 0.0 copy-done
  1.4 0.7 copy.7.of
  2.0 64.4 %shard_map.55 = bf16[1024,512]{1,0:T(8,128)(2,1)} custom-call(s32[8,2]{1,0:T(8,128)} %copy.6.af, s32[1,16]{1,0:T(1,128)} %bitcast.7, s32[8,4]{1,0:T(8,128)} %copy.7.of, bf16[1024,256]{1,0:T(8,128)(2,1)} %bitcast.4, bf16[128,2048]{1,0:T(8,128)(2,1)} %bitcast.5), custom_call_target="tpu_custom_call" | custom-call | tf_op jit(solution)/shard_map/pallas_call | solution.py:241
  66.5 2.3 %copy.9 = bf16[1024,512]{1,0:T(8,128)(2,1)} copy(bf16[1024,512]{1,0:T(8,128)(2,1)} %shard_map.55) | data formatting | bytes 2097152
Async XLA Ops:
  0.0 0.7 copy-start.1
  0.7 0.7 copy-start

commit v2 on v1

--- a/solution.py
+++ b/solution.py
@@ -116,45 +116,18 @@
     bbuf[p, pl.ds(pl.multiple_of(r * kb, kb), kb)] = bsl[p]
     others(r, n_r, lambda rr: by_copy(p, rr).start())
 
-    for d in range(1, n_p):
-        @pl.loop(0, nch)
-        def _(ch):
-            @pl.when(p >= d)
-            def _():
-                g = p - d
-                arrived(abuf.at[g, c, ch], zr.at[g, ch])
-
-                @pl.when(p < n_p - 1)
-                def _():
-                    z_copy(g, ch, p + 1, zsr).start()
-
-                forward(g, ch)
-
-            @pl.when(p + d < n_p)
-            def _():
-                g = p + d
-                arrived(abuf.at[g, c, ch], zr.at[g, ch])
-
-                @pl.when(p > 0)
-                def _():
-                    z_copy(g, ch, p - 1, zsl).start()
-
-                forward(g, ch)
-
-        def pass_b(g):
-            arrived(bbuf.at[g, pl.ds(pl.multiple_of(r * kb, kb), kb)], bzr.at[g])
-            others(r, n_r, lambda rr: by_copy(g, rr).start())
-
+    acc[...] = jnp.zeros_like(acc)
+    dacc[...] = jnp.ones_like(dacc)
+
+    def by_side(d, f):
         @pl.when(p >= d)
         def _():
-            pass_b(p - d)
-
-        @pl.when(p + d < n_p)
-        def _():
-            pass_b(p + d)
-
-    acc[...] = jnp.zeros_like(acc)
-    dacc[...] = jnp.ones_like(dacc)
+            f(p - d)
+
+        if d:
+            @pl.when(p + d < n_p)
+            def _():
+                f(p + d)
 
     def block(g, cc, ch):
         left = abuf[g, cc, ch]
@@ -165,39 +138,56 @@
             left, jnp.ones((ka, 128), jnp.bfloat16), preferred_element_type=jnp.float32
         )
 
-    def by_side(f):
-        for d in range(n_p):
-            @pl.when(p >= d)
-            def _():
-                f(p - d)
-
-            if d:
-                @pl.when(p + d < n_p)
-                def _():
-                    f(p + d)
-
-    def own(g):
-        def wait_b(rr):
-            arrived(bbuf.at[g, pl.ds(pl.multiple_of(rr * kb, kb), kb)], byr.at[g, rr])
-
-        others(r, n_r, wait_b)
-
+    def own(d, ch):
+        def one(g):
+            @pl.when(ch == 0)
+            def _():
+                others(r, n_r, lambda rr: arrived(
+                    bbuf.at[g, pl.ds(pl.multiple_of(rr * kb, kb), kb)], byr.at[g, rr]))
+
+            block(g, c, ch)
+
+        by_side(d, one)
+
+    def crossed(d, ch):
+        def one(g):
+            def from_col(cc):
+                arrived(abuf.at[g, cc, ch], xr.at[g, cc, ch])
+                block(g, cc, ch)
+
+            others(c, n_c, from_col)
+
+        by_side(d, one)
+
+    for d in range(1, n_p + 2):
         @pl.loop(0, nch)
         def _(ch):
-            block(g, c, ch)
-
-    by_side(own)
-
-    def crossed(g):
-        def one(cc):
-            @pl.loop(0, nch)
-            def _(ch):
-                arrived(abuf.at[g, cc, ch], xr.at[g, cc, ch])
-                block(g, cc, ch)
-
-        others(c, n_c, one)
-
-    by_side(crossed)
+            def pass_a(g):
+                arrived(abuf.at[g, c, ch], zr.at[g, ch])
+
+                @pl.when((g < p) & (p < n_p - 1))
+                def _():
+                    z_copy(g, ch, p + 1, zsr).start()
+
+                @pl.when((g > p) & (p > 0))
+                def _():
+                    z_copy(g, ch, p - 1, zsl).start()
+
+                forward(g, ch)
+
+            if d < n_p:
+                by_side(d, pass_a)
+            if d <= n_p:
+                own(d - 1, ch)
+            if d >= 2:
+                crossed(d - 2, ch)
+
+        def pass_b(g):
+            arrived(bbuf.at[g, pl.ds(pl.multiple_of(r * kb, kb), kb)], bzr.at[g])
+            others(r, n_r, lambda rr: by_copy(g, rr).start())
+
+        if d < n_p:
+            by_side(d, pass_b)
 
     @pl.loop(0, of.shape[0])
     def _(i):

time: 68.9 us -> 67.3 us (0.977)
  Pallas kernels: 64.4 us -> 62.8 us
    pallas_call x1, Pallas kernels: 64.4 us -> 62.8 us  [shards(): pl.pallas_call(functools.partial(kernel, n_r, n_c, n_p, nch, float(wide *...]
where the time goes in v2:
time: 67.3 us; the launch traced here: 67.1 us
  Pallas kernels  62.8 us (93%)
  local copies, waits for them, and re-layouts  4.29 us (6%)
    pallas_call x1, Pallas kernels, shards(): pl.pallas_call(functools.partial(kernel, n_r, n_c, n_p, nch, float(wide *...  62.8 us
    unnamed x6, local copies, waits for them, and re-layouts  3.62 us

profile of v2, /device:TPU:1, one launch (start us, length us, event | category | flops | bytes accessed | tf_op | source)
XLA Modules:
  0.0 67.1 jit_solution(10904040880549406060)
XLA Ops:
  0.0 0.0 copy-start.1
  0.0 0.7 %copy-done.1 = s32[1,8,2]{1,2,0:T(2,128)S(1)} copy-done((s32[1,8,2]{1,2,0:T(2,128)S(1)}, s32[1,8,2]{1,2,0:T(2,128)}, u32[]{:S(2)}) %copy-start.1) | copy-done | bytes 88
  0.7 0.0 copy-start
  0.7 0.7 %copy.6.af = s32[8,2]{1,0:T(8,128)} copy(s32[8,2]{0,1:T(2,128)S(1)} %bitcast.6) | data formatting | bytes 128 | tf_op jit(solution)/shard_map/squeeze | solution.py:254
  1.4 0.0 copy-done
  1.4 0.7 copy.7.of
  2.0 62.8 %shard_map.55 = bf16[1024,512]{1,0:T(8,128)(2,1)} custom-call(s32[8,2]{1,0:T(8,128)} %copy.6.af, s32[1,16]{1,0:T(1,128)} %bitcast.7, s32[8,4]{1,0:T(8,128)} %copy.7.of, bf16[1024,256]{1,0:T(8,128)(2,1)} %bitcast.4, bf16[128,2048]{1,0:T(8,128)(2,1)} %bitcast.5), custom_call_target="tpu_custom_call" | custom-call | tf_op jit(solution)/shard_map/pallas_call | solution.py:231
  64.8 2.3 %copy.9 = bf16[1024,512]{1,0:T(8,128)(2,1)} copy(bf16[1024,512]{1,0:T(8,128)(2,1)} %shard_map.55) | data formatting | bytes 2097152
Async XLA Ops:
  0.0 0.7 %copy-start.1 = (s32[1,8,2]{1,2,0:T(2,128)S(1)}, s32[1,8,2]{1,2,0:T(2,128)}, u32[]{:S(2)}) copy-start(s32[1,8,2]{1,2,0:T(2,128)} %param.6) | copy-start | bytes 196
  0.7 0.7 %copy-start = (s32[8,4]{0,1:T(4,128)S(1)}, s32[8,4]{0,1:T(4,128)}, u32[]{:S(2)}) copy-start(s32[8,4]{0,1:T(4,128)} %param.9) | copy-start | bytes 388

commit v3 on v0

v3 whole, which is shorter than its diff:
```python
import functools

import jax
import jax.numpy as jnp
from jax import lax
from jax.experimental import pallas as pl
from jax.experimental.pallas import tpu as pltpu
from jax.sharding import PartitionSpec as P

MESH = pl.DeviceIdType.MESH


def kernel(
    n_r, n_c, n_p, nch, factor,
    af, bf, of, a, b, out,
    abuf, bm, bsl, bbuf, dego, degr, acc, dacc, obuf, oin,
    zr, zsl, zsr, xr, xs, ts, bzr, bzs, bes, byr, bys, dr, ds, orecv, osend,
):
    r, c, p = lax.axis_index("row"), lax.axis_index("col"), lax.axis_index("rep")
    rows, ka = a.shape
    kb = b.shape[0]
    width = rows // af.shape[0]
    cols = out.shape[1]
    ch_rows = rows // nch
    per_ch = ch_rows // width
    half = nch // 2
    last = n_p - 1
    is_end = (p == 0) | (p == last)
    is_mid = (p > 0) & (p < last)
    upper = lax.div(p, n_p // 2)
    end = upper * last
    helper = 1 + upper * (last - 2)

    barrier = pltpu.get_barrier_semaphore()
    for axis, mine, count in (("row", r, n_r), ("col", c, n_c), ("rep", p, n_p)):
        for o in range(1, count):
            pl.semaphore_signal(
                barrier, inc=1, device_id={axis: lax.rem(mine + o, count)}, device_id_type=MESH
            )

    for i in range(bf.shape[0]):
        for j in range(bf.shape[1]):
            at = (slice(i * width, (i + 1) * width), slice(j * width, (j + 1) * width))
            bm[at] = (b[at].astype(jnp.float32) * bf[i, j].astype(jnp.float32)).astype(jnp.bfloat16)
    dego[...] = jnp.dot(
        bm[...], jnp.ones((bm.shape[1], 128), jnp.bfloat16), preferred_element_type=jnp.float32
    )
    for i in range(af.shape[0]):
        ch, off = divmod(i * width, ch_rows)
        for j in range(af.shape[1]):
            tile = a[i * width:(i + 1) * width, j * width:(j + 1) * width].astype(jnp.float32)
            abuf[p, c, ch, off:off + width, j * width:(j + 1) * width] = (
                tile * af[i, j].astype(jnp.float32)
            ).astype(jnp.bfloat16)

    pl.semaphore_wait(barrier, n_r + n_c + n_p - 3)

    def remote(src, dst, send, recv, **to):
        return pltpu.make_async_remote_copy(
            src_ref=src, dst_ref=dst, send_sem=send, recv_sem=recv,
            device_id=to, device_id_type=MESH)

    def arrived(ref, sem):
        pltpu.make_async_copy(ref, ref, sem).wait()

    def others(mine, count, f):
        @pl.loop(1, count)
        def _(o):
            f(lax.rem(mine + o, count))

    def start(copy):
        copy.start()

    def wait_send(copy):
        copy.wait_send()

    def z_copies(g, ch, act):
        block = abuf.at[g, c, ch]

        @pl.when((g >= p) & (p > 0) & ((p > 1) | (ch >= half)))
        def _():
            act(remote(block, block, zsl.at[g, ch], zr.at[g, ch], rep=p - 1))

        @pl.when((g <= p) & (p < last) & ((p < last - 1) | (ch >= half)))
        def _():
            act(remote(block, block, zsr.at[g, ch], zr.at[g, ch], rep=p + 1))

    def x_copies(g, ch, act):
        block = abuf.at[g, c, ch]

        @pl.when((g == p) | (is_mid & (g != end)) | (is_end & (ch >= half)))
        def _():
            others(c, n_c, lambda cc: act(
                remote(block, block, xs.at[g, cc, ch], xr.at[g, c, ch], col=cc)))

    def turn_copies(ch, act, wait):
        def one(cc):
            block = abuf.at[p, cc, ch]
            if wait:
                arrived(block, xr.at[p, cc, ch])
            act(remote(block, block, ts.at[cc, ch], xr.at[p, cc, ch], rep=helper))

        others(c, n_c, one)

    def b_rows(slot, g, rr):
        return bbuf.at[slot, g, pl.ds(pl.multiple_of(rr * kb, kb), kb)]

    def bz_copies(act):
        for pp, ee in ((1, 0), (last - 1, last)):
            @pl.when(p != pp)
            def _():
                for slot, part in ((0, pp), (1, ee)):
                    act(remote(
                        bsl.at[part], b_rows(slot, p, r), bzs.at[slot, pp], bzr.at[slot, p], rep=pp))

    def be_copy(g):
        return remote(b_rows(1, g, r), b_rows(0, g, r), bes.at[g], bzr.at[0, g], rep=end)

    def flip(index, bit):
        return index + bit - 2 * bit * lax.rem(lax.div(index, bit), 2)

    steps = []
    held = [()]
    bit = n_r // 2
    while bit:
        steps.append((bit, list(held)))
        held += [flips + (bit,) for flips in held]
        bit //= 2

    def flipped(flips):
        index = r
        for bit in flips:
            index = flip(index, bit)
        return index

    def by_copies(slot, g, step, act):
        bit, blocks = steps[step]
        for flips in blocks:
            rr = flipped(flips)
            block = b_rows(slot, g, rr)
            act(remote(block, block, bys.at[slot, g, step, rr], byr.at[slot, g, rr], row=flip(r, bit)))

    def by_arrived(slot, g, step):
        bit, blocks = steps[step]
        for flips in blocks:
            rr = flipped(flips + (bit,))
            arrived(b_rows(slot, g, rr), byr.at[slot, g, rr])

    def each_slot(f):
        f(0)

        @pl.when(is_mid)
        def _():
            f(1)

    def pass_b(g):
        def one(slot):
            @pl.when(g != p)
            def _():
                arrived(b_rows(slot, g, r), bzr.at[slot, g])

            by_copies(slot, g, 0, start)
            if slot == 1:
                @pl.when(g != end)
                def _():
                    be_copy(g).start()

        each_slot(one)

    def relay_b(g):
        def one(slot):
            for step in range(1, len(steps)):
                by_arrived(slot, g, step - 1)
                by_copies(slot, g, step, start)

        each_slot(one)

    def by_side(d, f):
        @pl.when(p >= d)
        def _():
            f(p - d)

        @pl.when(p + d < n_p)
        def _():
            f(p + d)

    def pass_a(d, low, high):
        @pl.loop(low, high)
        def _(ch):
            def one(g):
                arrived(abuf.at[g, c, ch], zr.at[g, ch])
                z_copies(g, ch, start)
                x_copies(g, ch, start)

            by_side(d, one)

    def send_own(low, high):
        @pl.loop(low, high)
        def _(ch):
            z_copies(p, ch, start)
            x_copies(p, ch, start)

    def deg_copy(cc):
        return remote(dego, degr.at[c], ds.at[cc], dr.at[c], col=cc)

    others(c, n_c, lambda cc: deg_copy(cc).start())
    send_own(0, half)

    deg = dacc.at[pl.ds(0, kb)]
    deg[...] = 1.0 + dego[...]

    def add_deg(cc):
        arrived(degr.at[cc], dr.at[cc])
        deg[...] += degr[cc]

    others(c, n_c, add_deg)
    for t in range(bm.shape[1] // 128):
        pp, off = divmod(t * 128, cols)
        bsl[pp, :, off:off + 128] = (
            bm[:, t * 128:(t + 1) * 128].astype(jnp.float32) / deg[...]
        ).astype(jnp.bfloat16)
    bz_copies(start)
    mine = pl.ds(pl.multiple_of(r * kb, kb), kb)
    bbuf[0, p, mine] = bsl[p]

    @pl.when(is_mid)
    def _():
        bbuf[1, p, mine] = bsl[end]

    pass_b(p)
    send_own(half, nch)

    def chunk(ch, slots):
        acc[...] = jnp.zeros_like(acc)
        dacc[...] = jnp.ones_like(dacc)
        top = dacc.at[pl.ds(0, ch_rows)]
        for g in range(n_p):
            def one(cc):
                left = abuf[g, cc, ch]
                for slot in range(slots):
                    right = bbuf[slot, g, pl.ds(pl.multiple_of(cc * ka, ka), ka)]
                    acc[slot] += jnp.dot(left, right, preferred_element_type=jnp.float32)
                top[...] += jnp.dot(
                    left, jnp.ones((ka, 128), jnp.bfloat16), preferred_element_type=jnp.float32
                )

            def from_col(cc):
                @pl.when(is_mid | (p != g))
                def _():
                    arrived(abuf.at[g, cc, ch], xr.at[g, cc, ch])

                one(cc)

            one(c)
            others(c, n_c, from_col)
        for i in range(per_ch):
            part = slice(i * width, (i + 1) * width)
            scale = factor / dacc[part]
            at = pl.ds(pl.multiple_of(ch * ch_rows + i * width, width), width)
            for j in range(of.shape[1]):
                tile = slice(j * width, (j + 1) * width)
                flag = of[ch * per_ch + i, j].astype(jnp.float32)
                out[at, tile] = (acc[0, part, tile] * (scale * flag)).astype(jnp.bfloat16)
                if slots == 2:
                    obuf[ch, part, tile] = (acc[1, part, tile] * scale).astype(jnp.bfloat16)

    def o_copy(ch):
        return remote(obuf.at[ch], oin.at[ch], osend.at[ch], orecv.at[ch], rep=end)

    def done_b():
        for g in range(n_p):
            each_slot(lambda slot: by_arrived(slot, g, len(steps) - 1))

    @pl.when(is_end)
    def _():
        def turn(low, high):
            @pl.loop(low, high)
            def _(ch):
                turn_copies(ch, start, True)

        turn(0, half)
        relay_b(p)
        turn(half, nch)
        for d in range(1, n_p):
            by_side(d, pass_b)
            pass_a(d, half, nch)
            by_side(d, relay_b)

    @pl.when(is_mid)
    def _():
        pass_a(1, 0, half)
        relay_b(p)
        by_side(1, pass_b)
        for d in range(2, n_p - 1):
            pass_a(d, 0, half)
            by_side(d - 1, relay_b)
            by_side(d, pass_b)
        pass_a(1, half, nch)
        by_side(n_p - 2, relay_b)

    done_b()

    @pl.when(is_mid)
    def _():
        @pl.loop(0, half)
        def _(ch):
            chunk(ch, 2)
            o_copy(ch).start()

        for d in range(2, n_p - 1):
            pass_a(d, half, nch)

    @pl.loop(half, nch)
    def _(ch):
        chunk(ch, 1)

    @pl.when(is_end)
    def _():
        @pl.loop(0, half)
        def _(ch):
            arrived(oin.at[ch], orecv.at[ch])
            for i in range(per_ch):
                at = pl.ds(pl.multiple_of(ch * ch_rows + i * width, width), width)
                for j in range(of.shape[1]):
                    tile = slice(j * width, (j + 1) * width)
                    flag = of[ch * per_ch + i, j].astype(jnp.float32)
                    part = oin[ch, i * width:(i + 1) * width, tile].astype(jnp.float32)
                    out[at, tile] = (part * flag).astype(jnp.bfloat16)

    others(c, n_c, lambda cc: deg_copy(cc).wait_send())
    bz_copies(wait_send)

    @pl.loop(0, n_p)
    def _(g):
        def sent(slot):
            for step in range(len(steps)):
                by_copies(slot, g, step, wait_send)
            if slot == 1:
                @pl.when(g != end)
                def _():
                    be_copy(g).wait_send()

        each_slot(sent)

        @pl.loop(0, nch)
        def _(ch):
            @pl.when((g == p) | is_mid | (ch >= half))
            def _():
                z_copies(g, ch, wait_send)
                x_copies(g, ch, wait_send)

    @pl.when(is_end)
    def _():
        @pl.loop(0, nch)
        def _(ch):
            turn_copies(ch, wait_send, False)

    @pl.when(is_mid)
    def _():
        @pl.loop(0, half)
        def _(ch):
            o_copy(ch).wait_send()


def shards(a_weights, a_flags, b_weights, b_flags, out_flags):
    n_r, n_c, n_p = (lax.axis_size(axis) for axis in ("row", "col", "rep"))
    _, rows, ka = a_weights.shape
    _, kb, wide = b_weights.shape
    cols = wide // n_p
    nch = max(2, 16 // n_c)
    dma = pltpu.SemaphoreType.DMA
    smem = pl.BlockSpec(memory_space=pltpu.SMEM)
    vmem = pl.BlockSpec(memory_space=pltpu.VMEM)
    return pl.pallas_call(
        functools.partial(kernel, n_r, n_c, n_p, nch, float(wide * n_c)),
        out_shape=jax.ShapeDtypeStruct((rows, cols), jnp.bfloat16),
        in_specs=[smem] * 3 + [vmem] * 2,
        out_specs=vmem,
        scratch_shapes=[
            pltpu.VMEM((n_p, n_c, nch, rows // nch, ka), jnp.bfloat16),
            pltpu.VMEM((kb, wide), jnp.bfloat16),
            pltpu.VMEM((n_p, kb, cols), jnp.bfloat16),
            pltpu.VMEM((2, n_p, n_r * kb, cols), jnp.bfloat16),
            pltpu.VMEM((kb, 128), jnp.float32),
            pltpu.VMEM((n_c, kb, 128), jnp.float32),
            pltpu.VMEM((2, rows // nch, cols), jnp.float32),
            pltpu.VMEM((max(kb, rows // nch), 128), jnp.float32),
            pltpu.VMEM((nch // 2, rows // nch, cols), jnp.bfloat16),
            pltpu.VMEM((nch // 2, rows // nch, cols), jnp.bfloat16),
            dma((n_p, nch)), dma((n_p, nch)), dma((n_p, nch)),
            dma((n_p, n_c, nch)), dma((n_p, n_c, nch)), dma((n_c, nch)),
            dma((2, n_p)), dma((2, n_p)), dma((n_p,)),
            dma((2, n_p, n_r)), dma((2, n_p, n_r.bit_length(), n_r)),
            dma((n_c,)), dma((n_c,)),
            dma((nch // 2,)), dma((nch // 2,)),
        ],
        compiler_params=pltpu.CompilerParams(
            collective_id=0, has_side_effects=True, vmem_limit_bytes=56 * 2**20
        ),
    )(a_flags[0], b_flags[0], out_flags, a_weights[0], b_weights[0])


def solution(mesh):
    return jax.shard_map(
        shards,
        mesh=mesh,
        in_specs=(
            P("rep", "row", "col"),
            P("rep", "row", "col"),
            P("rep", "row", "col"),
            P("rep", "row", "col"),
            P("row", ("col", "rep")),
        ),
        out_specs=P("row", ("col", "rep")),
        check_vma=False,
    )
```

time: 171 us -> 79.5 us (0.46)
  waiting for transfers between devices: 118 us -> 0 us
  Pallas kernels: 0 us -> 74.1 us
  blocking collectives: 22.6 us -> 0 us
  between operations: 13.2 us -> 0.01 us
  matrix products: 6.19 us -> 0 us
  other arithmetic: 4.51 us -> 0 us
    reduce_scatter x1 -> x0, waiting for transfers between devices: 75.8 us -> none  [shards(): lax.psum_scatter(partial_sum.astype(jnp.bfloat16), 'rep', scatter_dimensi...]
    pallas_call x0 -> x1, Pallas kernels: none -> 74.1 us  [shards(): pl.pallas_call(functools.partial(kernel, n_r, n_c, n_p, nch, float(wide *...]
    all_gather x2 -> x0, waiting for transfers between devices: 42 us -> none  [the longest x1 24.6 us: shards(): lax.all_gather(walk_b, 'row', axis=1, tiled=True)[0]]
    psum x2 -> x0, blocking collectives: 22.6 us -> none  [the longest x1 18.8 us: shards(): lax.psum(jnp.sum(a_masked, axis=(0, 2), dtype=jnp.float32), ('col', 'rep'))]
    dot_general x1 -> x0, matrix products: 6.19 us -> none  [shards(): jnp.dot(left_rows, lax.all_gather(walk_b, 'row', axis=1, tiled=True)[0],...]
    broadcast_in_dim x4 -> x0, local copies, waits for them, and re-layouts: 4.25 us -> none  [expand(): return jnp.repeat(jnp.repeat(flags, width, axis=-2), width, axis=-1)]
    convert_element_type x6 -> x0, other arithmetic: 4.09 us -> none  [the longest x1 1.39 us: shards(): (factor * summed * expand(out_flags, width).astype(jnp.float32)).astype(j...]
    unnamed x10 -> x6, local copies, waits for them, and re-layouts: 0.68 us -> 3.62 us
  transfers between devices with their start and end apart: 3 -> 0, of which waited for: 3 -> 0; matrix products, arithmetic and copies ran while one was open for 1% -> 0% of each run, Pallas kernels for 0% -> 0%
where the time goes in v3:
time: 79.5 us; the launch traced here: 78.4 us
  Pallas kernels  74.1 us (93%)
  local copies, waits for them, and re-layouts  4.29 us (5%)
    pallas_call x1, Pallas kernels, shards(): pl.pallas_call(functools.partial(kernel, n_r, n_c, n_p, nch, float(wide *...  74.1 us
    unnamed x6, local copies, waits for them, and re-layouts  3.62 us

profile of v3, /device:TPU:1, one launch (start us, length us, event | category | flops | bytes accessed | tf_op | source)
XLA Modules:
  0.0 78.4 jit_solution(6229748808090779737)
XLA Ops:
  0.0 0.0 copy-start.1
  0.0 0.7 copy-done.1
  0.7 0.0 copy-start
  0.7 0.7 copy.6.af
  1.4 0.0 copy-done
  1.4 0.7 copy.7.of
  2.0 74.1 %shard_map.55 = bf16[1024,512]{1,0:T(8,128)(2,1)} custom-call(s32[8,2]{1,0:T(8,128)} %copy.6.af, s32[1,16]{1,0:T(1,128)} %bitcast.7, s32[8,4]{1,0:T(8,128)} %copy.7.of, bf16[1024,256]{1,0:T(8,128)(2,1)} %bitcast.4, bf16[128,2048]{1,0:T(8,128)(2,1)} %bitcast.5), custom_call_target="tpu_custom_call" | custom-call | tf_op jit(solution)/shard_map/pallas_call | solution.py:374
  76.1 2.3 %copy.9 = bf16[1024,512]{1,0:T(8,128)(2,1)} copy(bf16[1024,512]{1,0:T(8,128)(2,1)} %shard_map.55) | data formatting | bytes 2097152
Async XLA Ops:
  0.0 0.7 copy-start.1
  0.7 0.7 copy-start

commit v4 on v3

--- a/solution.py
+++ b/solution.py
@@ -23,7 +23,7 @@
     cols = out.shape[1]
     ch_rows = rows // nch
     per_ch = ch_rows // width
-    half = nch // 2
+    half = obuf.shape[0]
     last = n_p - 1
     is_end = (p == 0) | (p == last)
     is_mid = (p > 0) & (p < last)
@@ -194,17 +194,17 @@
 
             by_side(d, one)
 
-    def send_own(low, high):
+    def send_own(copies, low, high):
         @pl.loop(low, high)
         def _(ch):
-            z_copies(p, ch, start)
-            x_copies(p, ch, start)
+            copies(p, ch, start)
 
     def deg_copy(cc):
         return remote(dego, degr.at[c], ds.at[cc], dr.at[c], col=cc)
 
     others(c, n_c, lambda cc: deg_copy(cc).start())
-    send_own(0, half)
+    send_own(z_copies, 0, half)
+    send_own(x_copies, 0, nch)
 
     deg = dacc.at[pl.ds(0, kb)]
     deg[...] = 1.0 + dego[...]
@@ -228,7 +228,17 @@
         bbuf[1, p, mine] = bsl[end]
 
     pass_b(p)
-    send_own(half, nch)
+
+    def turn(low, high):
+        @pl.when(is_end)
+        def _():
+            @pl.loop(low, high)
+            def _(ch):
+                turn_copies(ch, start, True)
+
+    turn(0, half)
+    send_own(z_copies, half, nch)
+    turn(half, nch)
 
     def chunk(ch, slots):
         acc[...] = jnp.zeros_like(acc)
@@ -273,18 +283,24 @@
 
     @pl.when(is_end)
     def _():
-        def turn(low, high):
-            @pl.loop(low, high)
-            def _(ch):
-                turn_copies(ch, start, True)
-
-        turn(0, half)
         relay_b(p)
-        turn(half, nch)
-        for d in range(1, n_p):
+        for d in range(1, n_p - 1):
             by_side(d, pass_b)
             pass_a(d, half, nch)
             by_side(d, relay_b)
+        by_side(n_p - 1, pass_b)
+        by_side(n_p - 1, relay_b)
+        done_b()
+
+        @pl.loop(half, nch)
+        def _(ch):
+            pass_a(n_p - 1, ch, ch + 1)
+
+            @pl.when(ch > half)
+            def _():
+                chunk(ch - 1, 1)
+
+        chunk(nch - 1, 1)
 
     @pl.when(is_mid)
     def _():
@@ -295,24 +311,21 @@
             pass_a(d, 0, half)
             by_side(d - 1, relay_b)
             by_side(d, pass_b)
-        pass_a(1, half, nch)
+        pass_a(1, half, half + 1)
         by_side(n_p - 2, relay_b)
-
-    done_b()
-
-    @pl.when(is_mid)
-    def _():
+        pass_a(1, half + 1, nch)
+        for d in range(2, n_p - 1):
+            pass_a(d, half, nch)
+        done_b()
+
         @pl.loop(0, half)
         def _(ch):
             chunk(ch, 2)
             o_copy(ch).start()
 
-        for d in range(2, n_p - 1):
-            pass_a(d, half, nch)
-
-    @pl.loop(half, nch)
-    def _(ch):
-        chunk(ch, 1)
+        @pl.loop(half, nch)
+        def _(ch):
+            chunk(ch, 1)
 
     @pl.when(is_end)
     def _():
@@ -367,7 +380,8 @@
     _, rows, ka = a_weights.shape
     _, kb, wide = b_weights.shape
     cols = wide // n_p
-    nch = max(2, 16 // n_c)
+    nch = max(2, 8 // n_c)
+    helped = max(1, nch // 4)
     dma = pltpu.SemaphoreType.DMA
     smem = pl.BlockSpec(memory_space=pltpu.SMEM)
     vmem = pl.BlockSpec(memory_space=pltpu.VMEM)
@@ -385,14 +399,14 @@
             pltpu.VMEM((n_c, kb, 128), jnp.float32),
             pltpu.VMEM((2, rows // nch, cols), jnp.float32),
             pltpu.VMEM((max(kb, rows // nch), 128), jnp.float32),
-            pltpu.VMEM((nch // 2, rows // nch, cols), jnp.bfloat16),
-            pltpu.VMEM((nch // 2, rows // nch, cols), jnp.bfloat16),
+            pltpu.VMEM((helped, rows // nch, cols), jnp.bfloat16),
+            pltpu.VMEM((helped, rows // nch, cols), jnp.bfloat16),
             dma((n_p, nch)), dma((n_p, nch)), dma((n_p, nch)),
             dma((n_p, n_c, nch)), dma((n_p, n_c, nch)), dma((n_c, nch)),
             dma((2, n_p)), dma((2, n_p)), dma((n_p,)),
             dma((2, n_p, n_r)), dma((2, n_p, n_r.bit_length(), n_r)),
             dma((n_c,)), dma((n_c,)),
-            dma((nch // 2,)), dma((nch // 2,)),
+            dma((helped,)), dma((helped,)),
         ],
         compiler_params=pltpu.CompilerParams(
             collective_id=0, has_side_effects=True, vmem_limit_bytes=56 * 2**20

time: 79.5 us -> 71.1 us (0.89); the launches traced: 78.4 us -> 70.8 us
  Pallas kernels: 74.1 us -> 66.5 us
    pallas_call x1, Pallas kernels: 74.1 us -> 66.5 us  [shards(): pl.pallas_call(functools.partial(kernel, n_r, n_c, n_p, nch, float(wide *...]
where the time goes in v4:
time: 71.1 us; the launch traced here: 70.8 us
  Pallas kernels  66.5 us (94%)
  local copies, waits for them, and re-layouts  4.29 us (6%)
    pallas_call x1, Pallas kernels, shards(): pl.pallas_call(functools.partial(kernel, n_r, n_c, n_p, nch, float(wide *...  66.5 us
    unnamed x6, local copies, waits for them, and re-layouts  3.62 us

profile of v4, /device:TPU:1, one launch (start us, length us, event | category | flops | bytes accessed | tf_op | source)
XLA Modules:
  0.0 70.8 jit_solution(13382326006670375787)
XLA Ops:
  0.0 0.0 copy-start.1
  0.0 0.7 copy-done.1
  0.7 0.0 copy-start
  0.7 0.7 copy.6.af
  1.4 0.0 copy-done
  1.4 0.7 copy.7.of
  2.0 66.5 %shard_map.55 = bf16[1024,512]{1,0:T(8,128)(2,1)} custom-call(s32[8,2]{1,0:T(8,128)} %copy.6.af, s32[1,16]{1,0:T(1,128)} %bitcast.7, s32[8,4]{1,0:T(8,128)} %copy.7.of, bf16[1024,256]{1,0:T(8,128)(2,1)} %bitcast.4, bf16[128,2048]{1,0:T(8,128)(2,1)} %bitcast.5), custom_call_target="tpu_custom_call" | custom-call | tf_op jit(solution)/shard_map/pallas_call | solution.py:388
  68.6 2.3 %copy.9 = bf16[1024,512]{1,0:T(8,128)(2,1)} copy(bf16[1024,512]{1,0:T(8,128)(2,1)} %shard_map.55) | data formatting | bytes 2097152
Async XLA Ops:
  0.0 0.7 copy-start.1
  0.7 0.7 copy-start

commit v5 on v2

--- a/solution.py
+++ b/solution.py
@@ -11,17 +11,29 @@
 
 
 def kernel(
-    n_r, n_c, n_p, nch, factor,
-    af, bf, of, a, b, out,
-    abuf, bm, bsl, bbuf, dego, degr, acc, dacc,
-    zr, zsl, zsr, xr, xs, bzr, bzs, byr, bys, dr, ds,
+    n_r, n_c, n_p, nch,
+    af_in, bf_in, of_in, a_in, b_in, out,
+    af, bf, of, a, b, loads, abuf, bm, bsl, bbuf, dego, degr, acc, dacc,
+    zr, zsl, zsr, xr, xs, ts, bzr, bzs, byr, bys, dr, ds,
 ):
     r, c, p = lax.axis_index("row"), lax.axis_index("col"), lax.axis_index("rep")
     rows, ka = a.shape
     kb = b.shape[0]
-    width = rows // af.shape[0]
+    width = rows // af.shape[1]
     cols = out.shape[1]
     ch_rows = rows // nch
+    last = n_p - 1
+    turns = n_p >= 4
+    is_end = (p == 0) | (p == last)
+    inner = 1 + lax.div(p, n_p // 2) * (last - 2)
+
+    copies = [
+        pltpu.make_async_copy(src, dst, loads.at[k])
+        for k, (src, dst) in enumerate(
+            ((bf_in, bf), (b_in, b), (af_in, af), (a_in, a), (of_in, of)))
+    ]
+    for copy in copies:
+        copy.start()
 
     barrier = pltpu.get_barrier_semaphore()
     for axis, mine, count in (("row", r, n_r), ("col", c, n_c), ("rep", p, n_p)):
@@ -29,6 +41,9 @@
             pl.semaphore_signal(
                 barrier, inc=1, device_id={axis: lax.rem(mine + o, count)}, device_id_type=MESH
             )
+
+    for copy in copies:
+        copy.wait()
 
     for i in range(bf.shape[0]):
         for j in range(bf.shape[1]):
@@ -37,12 +52,12 @@
     dego[...] = jnp.dot(
         bm[...], jnp.ones((bm.shape[1], 128), jnp.bfloat16), preferred_element_type=jnp.float32
     )
-    for i in range(af.shape[0]):
+    for i in range(af.shape[1]):
         ch, off = divmod(i * width, ch_rows)
-        for j in range(af.shape[1]):
+        for j in range(af.shape[0]):
             tile = a[i * width:(i + 1) * width, j * width:(j + 1) * width].astype(jnp.float32)
             abuf[p, c, ch, off:off + width, j * width:(j + 1) * width] = (
-                tile * af[i, j].astype(jnp.float32)
+                tile * af[j, i].astype(jnp.float32)
             ).astype(jnp.bfloat16)
 
     pl.semaphore_wait(barrier, n_r + n_c + n_p - 3)
@@ -83,8 +98,30 @@
         def _(o):
             f(lax.rem(mine + o, count))
 
+    def crosses(g):
+        if not turns:
+            return g >= 0
+        return ((p != 1) | (g != 0)) & ((p != last - 1) | (g != last))
+
     def forward(g, ch):
-        others(c, n_c, lambda cc: x_copy(g, ch, cc).start())
+        @pl.when(crosses(g))
+        def _():
+            others(c, n_c, lambda cc: x_copy(g, ch, cc).start())
+
+    def turn_copy(cc, ch):
+        block = abuf.at[p, cc, ch]
+        return pltpu.make_async_remote_copy(
+            src_ref=block, dst_ref=block, send_sem=ts.at[cc, ch], recv_sem=xr.at[p, cc, ch],
+            device_id={"rep": inner}, device_id_type=MESH)
+
+    def turn(ch):
+        def one(cc):
+            arrived(abuf.at[p, cc, ch], xr.at[p, cc, ch])
+            turn_copy(cc, ch).start()
+
+        @pl.when(is_end)
+        def _():
+            others(c, n_c, one)
 
     others(c, n_c, lambda cc: deg_copy(cc).start())
 
@@ -152,7 +189,10 @@
     def crossed(d, ch):
         def one(g):
             def from_col(cc):
-                arrived(abuf.at[g, cc, ch], xr.at[g, cc, ch])
+                @pl.when((g != p) | ~is_end if turns else g >= 0)
+                def _():
+                    arrived(abuf.at[g, cc, ch], xr.at[g, cc, ch])
+
                 block(g, cc, ch)
 
             others(c, n_c, from_col)
@@ -177,6 +217,8 @@
 
             if d < n_p:
                 by_side(d, pass_a)
+            if d == 1 and turns:
+                turn(ch)
             if d <= n_p:
                 own(d - 1, ch)
             if d >= 2:
@@ -189,15 +231,22 @@
         if d < n_p:
             by_side(d, pass_b)
 
-    @pl.loop(0, of.shape[0])
+    @pl.loop(0, of.shape[1])
     def _(i):
         at = pl.ds(pl.multiple_of(i * width, width), width)
-        scale = factor / dacc[at]
-        for j in range(of.shape[1]):
+        scale = 1.0 / dacc[at]
+        for j in range(of.shape[0]):
             tile = slice(j * width, (j + 1) * width)
             out[at, tile] = (
-                acc[at, tile] * (scale * of[i, j].astype(jnp.float32))
+                acc[at, tile] * (scale * of[j, i].astype(jnp.float32))
             ).astype(jnp.bfloat16)
+
+    if turns:
+        @pl.when(is_end)
+        def _():
+            @pl.loop(0, nch)
+            def _(ch):
+                others(c, n_c, lambda cc: turn_copy(cc, ch).wait_send())
 
     others(c, n_c, lambda cc: deg_copy(cc).wait_send())
     others(p, n_p, lambda pp: bz_copy(pp).wait_send())
@@ -208,7 +257,9 @@
 
         @pl.loop(0, nch)
         def _(ch):
-            others(c, n_c, lambda cc: x_copy(g, ch, cc).wait_send())
+            @pl.when(crosses(g))
+            def _():
+                others(c, n_c, lambda cc: x_copy(g, ch, cc).wait_send())
 
             @pl.when((g >= p) & (p > 0))
             def _():
@@ -226,14 +277,16 @@
     cols = wide // n_p
     nch = max(1, 8 // n_c)
     dma = pltpu.SemaphoreType.DMA
-    smem = pl.BlockSpec(memory_space=pltpu.SMEM)
-    vmem = pl.BlockSpec(memory_space=pltpu.VMEM)
-    return pl.pallas_call(
-        functools.partial(kernel, n_r, n_c, n_p, nch, float(wide * n_c)),
+    operands = (a_flags[0].T, b_flags[0], out_flags.T, a_weights[0], b_weights[0])
+    density = pl.pallas_call(
+        functools.partial(kernel, n_r, n_c, n_p, nch),
         out_shape=jax.ShapeDtypeStruct((rows, cols), jnp.bfloat16),
-        in_specs=[smem] * 3 + [vmem] * 2,
-        out_specs=vmem,
+        in_specs=[pl.BlockSpec(memory_space=pl.ANY)] * 5,
+        out_specs=pl.BlockSpec(memory_space=pltpu.VMEM),
         scratch_shapes=[
+            *(pltpu.SMEM(x.shape, x.dtype) for x in operands[:3]),
+            *(pltpu.VMEM(x.shape, x.dtype) for x in operands[3:]),
+            dma((5,)),
             pltpu.VMEM((n_p, n_c, nch, rows // nch, ka), jnp.bfloat16),
             pltpu.VMEM((kb, wide), jnp.bfloat16),
             pltpu.VMEM((n_p, kb, cols), jnp.bfloat16),
@@ -243,7 +296,7 @@
             pltpu.VMEM((rows, cols), jnp.float32),
             pltpu.VMEM((rows, 128), jnp.float32),
             dma((n_p, nch)), dma((n_p, nch)), dma((n_p, nch)),
-            dma((n_p, n_c, nch)), dma((n_p, n_c, nch)),
+            dma((n_p, n_c, nch)), dma((n_p, n_c, nch)), dma((n_c, nch)),
             dma((n_p,)), dma((n_p,)),
             dma((n_p, n_r)), dma((n_p, n_r)),
             dma((n_c,)), dma((n_c,)),
@@ -251,7 +304,9 @@
         compiler_params=pltpu.CompilerParams(
             collective_id=0, has_side_effects=True, vmem_limit_bytes=56 * 2**20
         ),
-    )(a_flags[0], b_flags[0], out_flags, a_weights[0], b_weights[0])
+    )(*operands)
+    factor = jnp.float32(wide * n_c)
+    return (factor * density.astype(jnp.float32)).astype(jnp.bfloat16)
 
 
 def solution(mesh):

time: 67.3 us -> 64.3 us (0.955)
  local copies, waits for them, and re-layouts: 4.29 us -> 0 us
  other arithmetic: 0 us -> 2.39 us
  Pallas kernels: 62.8 us -> 61.7 us
    unnamed x6 -> x0, local copies, waits for them, and re-layouts: 3.62 us -> none
    convert_element_type x0 -> x1, other arithmetic: none -> 2.39 us  [shards(): return (factor * density.astype(jnp.float32)).astype(jnp.bfloat16)]
    pallas_call x1, Pallas kernels: 62.8 us -> 61.7 us  [shards(): pl.pallas_call(functools.partial(kernel, n_r, n_c, n_p, nch), out_shape=j...]
where the time goes in v5:
time: 64.3 us; the launch traced here: 64.1 us
  Pallas kernels  61.7 us (96%)
  other arithmetic  2.39 us (4%)
    pallas_call x1, Pallas kernels, shards(): pl.pallas_call(functools.partial(kernel, n_r, n_c, n_p, nch), out_shape=j...  61.7 us
    convert_element_type x1, other arithmetic, shards(): return (factor * density.astype(jnp.float32)).astype(jnp.bfloat16)  2.39 us

profile of v5, /device:TPU:1, one launch (start us, length us, event | category | flops | bytes accessed | tf_op | source)
XLA Modules:
  0.0 64.1 jit_solution(5990457067312873217)
XLA Ops:
  0.0 61.7 %shard_map.55 = bf16[1024,512]{1,0:T(8,128)(2,1)} custom-call(s32[2,8]{1,0:T(2,128)} %bitcast.10, s32[1,16]{1,0:T(1,128)} %bitcast.11, s32[4,8]{1,0:T(4,128)} %bitcast.9, bf16[1024,256]{1,0:T(8,128)(2,1)} %bitcast.7, bf16[128,2048]{1,0:T(8,128)(2,1)} %bitcast.8), custom_call_target="tpu_custom_call" | custom-call | tf_op jit(solution)/shard_map/pallas_call | solution.py:281
  61.7 2.4 %multiply_convert_fusion = bf16[1024,512]{1,0:T(8,128)(2,1)} fusion(bf16[1024,512]{1,0:T(8,128)(2,1)} %shard_map.55), kind=kLoop, calls=%fused_computation | loop fusion | flops 1572864 | bytes 2097152 | tf_op jit(solution)/shard_map/convert_element_type | solution.py:309

commit v6 on v5

--- a/solution.py
+++ b/solution.py
@@ -27,14 +27,6 @@
     is_end = (p == 0) | (p == last)
     inner = 1 + lax.div(p, n_p // 2) * (last - 2)
 
-    copies = [
-        pltpu.make_async_copy(src, dst, loads.at[k])
-        for k, (src, dst) in enumerate(
-            ((bf_in, bf), (b_in, b), (af_in, af), (a_in, a), (of_in, of)))
-    ]
-    for copy in copies:
-        copy.start()
-
     barrier = pltpu.get_barrier_semaphore()
     for axis, mine, count in (("row", r, n_r), ("col", c, n_c), ("rep", p, n_p)):
         for o in range(1, count):
@@ -42,7 +34,99 @@
                 barrier, inc=1, device_id={axis: lax.rem(mine + o, count)}, device_id_type=MESH
             )
 
+    copies = [
+        pltpu.make_async_copy(src, dst, loads.at[k])
+        for k, (src, dst) in enumerate(
+            ((af_in, af), (a_in, a), (bf_in, bf), (b_in, b), (of_in, of)))
+    ]
     for copy in copies:
+        copy.start()
+
+    for copy in copies[:2]:
+        copy.wait()
+
+    for i in range(af.shape[1]):
+        ch, off = divmod(i * width, ch_rows)
+        for j in range(af.shape[0]):
+            tile = a[i * width:(i + 1) * width, j * width:(j + 1) * width].astype(jnp.float32)
+            abuf[p, c, ch, off:off + width, j * width:(j + 1) * width] = (
+                tile * af[j, i].astype(jnp.float32)
+            ).astype(jnp.bfloat16)
+
+    pl.semaphore_wait(barrier, n_r + n_c + n_p - 3)
+
+    def deg_copy(cc):
+        return pltpu.make_async_remote_copy(
+            src_ref=dego, dst_ref=degr.at[c], send_sem=ds.at[cc], recv_sem=dr.at[c],
+            device_id={"col": cc}, device_id_type=MESH)
+
+    def z_copy(g, ch, to, send):
+        block = abuf.at[g, c, ch]
+        return pltpu.make_async_remote_copy(
+            src_ref=block, dst_ref=block, send_sem=send.at[g, ch], recv_sem=zr.at[g, ch],
+            device_id={"rep": to}, device_id_type=MESH)
+
+    def x_copy(g, ch, cc):
+        block = abuf.at[g, c, ch]
+        return pltpu.make_async_remote_copy(
+            src_ref=block, dst_ref=block, send_sem=xs.at[g, cc, ch], recv_sem=xr.at[g, c, ch],
+            device_id={"col": cc}, device_id_type=MESH)
+
+    def bz_copy(pp):
+        return pltpu.make_async_remote_copy(
+            src_ref=bsl.at[pp], dst_ref=bbuf.at[p, pl.ds(pl.multiple_of(r * kb, kb), kb)],
+            send_sem=bzs.at[pp], recv_sem=bzr.at[p], device_id={"rep": pp}, device_id_type=MESH)
+
+    def by_copy(g, rr):
+        block = bbuf.at[g, pl.ds(pl.multiple_of(r * kb, kb), kb)]
+        return pltpu.make_async_remote_copy(
+            src_ref=block, dst_ref=block, send_sem=bys.at[g, rr], recv_sem=byr.at[g, r],
+            device_id={"row": rr}, device_id_type=MESH)
+
+    def arrived(ref, sem):
+        pltpu.make_async_copy(ref, ref, sem).wait()
+
+    def others(mine, count, f):
+        @pl.loop(1, count)
+        def _(o):
+            f(lax.rem(mine + o, count))
+
+    def crosses(g):
+        if not turns:
+            return g >= 0
+        return ((p != 1) | (g != 0)) & ((p != last - 1) | (g != last))
+
+    def forward(g, ch):
+        @pl.when(crosses(g))
+        def _():
+            others(c, n_c, lambda cc: x_copy(g, ch, cc).start())
+
+    def turn_copy(cc, ch):
+        block = abuf.at[p, cc, ch]
+        return pltpu.make_async_remote_copy(
+            src_ref=block, dst_ref=block, send_sem=ts.at[cc, ch], recv_sem=xr.at[p, cc, ch],
+            device_id={"rep": inner}, device_id_type=MESH)
+
+    def turn(ch):
+        def one(cc):
+            arrived(abuf.at[p, cc, ch], xr.at[p, cc, ch])
+            turn_copy(cc, ch).start()
+
+        @pl.when(is_end)
+        def _():
+            others(c, n_c, one)
+
+    @pl.loop(0, nch)
+    def _(ch):
+        @pl.when(p > 0)
+        def _():
+            z_copy(p, ch, p - 1, zsl).start()
+
+        @pl.when(p < n_p - 1)
+        def _():
+            z_copy(p, ch, p + 1, zsr).start()
+
+    for copy in copies[2:]:
         copy.wait()
 
     for i in range(bf.shape[0]):
@@ -52,89 +136,10 @@
     dego[...] = jnp.dot(
         bm[...], jnp.ones((bm.shape[1], 128), jnp.bfloat16), preferred_element_type=jnp.float32
     )
-    for i in range(af.shape[1]):
-        ch, off = divmod(i * width, ch_rows)
-        for j in range(af.shape[0]):
-            tile = a[i * width:(i + 1) * width, j * width:(j + 1) * width].astype(jnp.float32)
-            abuf[p, c, ch, off:off + width, j * width:(j + 1) * width] = (
-                tile * af[j, i].astype(jnp.float32)
-            ).astype(jnp.bfloat16)
-
-    pl.semaphore_wait(barrier, n_r + n_c + n_p - 3)
-
-    def deg_copy(cc):
-        return pltpu.make_async_remote_copy(
-            src_ref=dego, dst_ref=degr.at[c], send_sem=ds.at[cc], recv_sem=dr.at[c],
-            device_id={"col": cc}, device_id_type=MESH)
-
-    def z_copy(g, ch, to, send):
-        block = abuf.at[g, c, ch]
-        return pltpu.make_async_remote_copy(
-            src_ref=block, dst_ref=block, send_sem=send.at[g, ch], recv_sem=zr.at[g, ch],
-            device_id={"rep": to}, device_id_type=MESH)
-
-    def x_copy(g, ch, cc):
-        block = abuf.at[g, c, ch]
-        return pltpu.make_async_remote_copy(
-            src_ref=block, dst_ref=block, send_sem=xs.at[g, cc, ch], recv_sem=xr.at[g, c, ch],
-            device_id={"col": cc}, device_id_type=MESH)
-
-    def bz_copy(pp):
-        return pltpu.make_async_remote_copy(
-            src_ref=bsl.at[pp], dst_ref=bbuf.at[p, pl.ds(pl.multiple_of(r * kb, kb), kb)],
-            send_sem=bzs.at[pp], recv_sem=bzr.at[p], device_id={"rep": pp}, device_id_type=MESH)
-
-    def by_copy(g, rr):
-        block = bbuf.at[g, pl.ds(pl.multiple_of(r * kb, kb), kb)]
-        return pltpu.make_async_remote_copy(
-            src_ref=block, dst_ref=block, send_sem=bys.at[g, rr], recv_sem=byr.at[g, r],
-            device_id={"row": rr}, device_id_type=MESH)
-
-    def arrived(ref, sem):
-        pltpu.make_async_copy(ref, ref, sem).wait()
-
-    def others(mine, count, f):
-        @pl.loop(1, count)
-        def _(o):
-            f(lax.rem(mine + o, count))
-
-    def crosses(g):
-        if not turns:
-            return g >= 0
-        return ((p != 1) | (g != 0)) & ((p != last - 1) | (g != last))
-
-    def forward(g, ch):
-        @pl.when(crosses(g))
-        def _():
-            others(c, n_c, lambda cc: x_copy(g, ch, cc).start())
-
-    def turn_copy(cc, ch):
-        block = abuf.at[p, cc, ch]
-        return pltpu.make_async_remote_copy(
-            src_ref=block, dst_ref=block, send_sem=ts.at[cc, ch], recv_sem=xr.at[p, cc, ch],
-            device_id={"rep": inner}, device_id_type=MESH)
-
-    def turn(ch):
-        def one(cc):
-            arrived(abuf.at[p, cc, ch], xr.at[p, cc, ch])
-            turn_copy(cc, ch).start()
-
-        @pl.when(is_end)
-        def _():
-            others(c, n_c, one)
-
     others(c, n_c, lambda cc: deg_copy(cc).start())
 
     @pl.loop(0, nch)
     def _(ch):
-        @pl.when(p > 0)
-        def _():
-            z_copy(p, ch, p - 1, zsl).start()
-
-        @pl.when(p < n_p - 1)
-        def _():
-            z_copy(p, ch, p + 1, zsr).start()
-
         forward(p, ch)
 
     def add_deg(cc):
@@ -199,40 +204,11 @@
 
         by_side(d, one)
 
-    for d in range(1, n_p + 2):
-        @pl.loop(0, nch)
-        def _(ch):
-            def pass_a(g):
-                arrived(abuf.at[g, c, ch], zr.at[g, ch])
-
-                @pl.when((g < p) & (p < n_p - 1))
-                def _():
-                    z_copy(g, ch, p + 1, zsr).start()
-
-                @pl.when((g > p) & (p > 0))
-                def _():
-                    z_copy(g, ch, p - 1, zsl).start()
-
-                forward(g, ch)
-
-            if d < n_p:
-                by_side(d, pass_a)
-            if d == 1 and turns:
-                turn(ch)
-            if d <= n_p:
-                own(d - 1, ch)
-            if d >= 2:
-                crossed(d - 2, ch)
-
-        def pass_b(g):
-            arrived(bbuf.at[g, pl.ds(pl.multiple_of(r * kb, kb), kb)], bzr.at[g])
-            others(r, n_r, lambda rr: by_copy(g, rr).start())
-
-        if d < n_p:
-            by_side(d, pass_b)
-
-    @pl.loop(0, of.shape[1])
-    def _(i):
+    def pass_b(g):
+        arrived(bbuf.at[g, pl.ds(pl.multiple_of(r * kb, kb), kb)], bzr.at[g])
+        others(r, n_r, lambda rr: by_copy(g, rr).start())
+
+    def finish(i):
         at = pl.ds(pl.multiple_of(i * width, width), width)
         scale = 1.0 / dacc[at]
         for j in range(of.shape[0]):
@@ -240,6 +216,45 @@
             out[at, tile] = (
                 acc[at, tile] * (scale * of[j, i].astype(jnp.float32))
             ).astype(jnp.bfloat16)
+
+    for d in range(1, n_p + 1):
+        if 1 < d < n_p:
+            by_side(d, pass_b)
+
+        @pl.loop(0, nch)
+        def _(ch):
+            def pass_a(g):
+                arrived(abuf.at[g, c, ch], zr.at[g, ch])
+
+                @pl.when((g < p) & (p < n_p - 1))
+                def _():
+                    z_copy(g, ch, p + 1, zsr).start()
+
+                @pl.when((g > p) & (p > 0))
+                def _():
+                    z_copy(g, ch, p - 1, zsl).start()
+
+                forward(g, ch)
+
+            if d < n_p:
+                by_side(d, pass_a)
+            if d == 1:
+                if turns:
+                    turn(ch)
+                own(0, ch)
+            if d == 2:
+                own(1, ch)
+                crossed(0, ch)
+            if 1 < d <= n_p:
+                crossed(d - 1, ch)
+            if 1 < d < n_p:
+                own(d, ch)
+            if d == n_p:
+                for i in range(ch_rows // width):
+                    finish(ch * (ch_rows // width) + i)
+
+        if d == 1:
+            by_side(1, pass_b)
 
     if turns:
         @pl.when(is_end)

time: 64.3 us -> 63.4 us (0.986)
  Pallas kernels: 61.7 us -> 60.8 us
    pallas_call x1, Pallas kernels: 61.7 us -> 60.8 us  [shards(): pl.pallas_call(functools.partial(kernel, n_r, n_c, n_p, nch), out_shape=j...]
where the time goes in v6:
time: 63.4 us; the launch traced here: 63.2 us
  Pallas kernels  60.8 us (96%)
  other arithmetic  2.39 us (4%)
    pallas_call x1, Pallas kernels, shards(): pl.pallas_call(functools.partial(kernel, n_r, n_c, n_p, nch), out_shape=j...  60.8 us
    convert_element_type x1, other arithmetic, shards(): return (factor * density.astype(jnp.float32)).astype(jnp.bfloat16)  2.39 us

profile of v6, /device:TPU:1, one launch (start us, length us, event | category | flops | bytes accessed | tf_op | source)
XLA Modules:
  0.0 63.2 jit_solution(2231543477953624635)
XLA Ops:
  0.0 60.8 %shard_map.55 = bf16[1024,512]{1,0:T(8,128)(2,1)} custom-call(s32[2,8]{1,0:T(2,128)} %bitcast.10, s32[1,16]{1,0:T(1,128)} %bitcast.11, s32[4,8]{1,0:T(4,128)} %bitcast.9, bf16[1024,256]{1,0:T(8,128)(2,1)} %bitcast.7, bf16[128,2048]{1,0:T(8,128)(2,1)} %bitcast.8), custom_call_target="tpu_custom_call" | custom-call | tf_op jit(solution)/shard_map/pallas_call | solution.py:296
  60.8 2.4 %multiply_convert_fusion = bf16[1024,512]{1,0:T(8,128)(2,1)} fusion(bf16[1024,512]{1,0:T(8,128)(2,1)} %shard_map.55), kind=kLoop, calls=%fused_computation | loop fusion | flops 1572864 | bytes 2097152 | tf_op jit(solution)/shard_map/convert_element_type | solution.py:324

commit v7 on v6

--- a/solution.py
+++ b/solution.py
@@ -293,10 +293,12 @@
     nch = max(1, 8 // n_c)
     dma = pltpu.SemaphoreType.DMA
     operands = (a_flags[0].T, b_flags[0], out_flags.T, a_weights[0], b_weights[0])
+    held = 2 * (rows * ka * (n_p * n_c + 1) + kb * wide * 3 + n_p * n_r * kb * cols + rows * cols)
+    held += 4 * (kb * 128 * (n_c + 1) + rows * (cols + 128))
     density = pl.pallas_call(
         functools.partial(kernel, n_r, n_c, n_p, nch),
         out_shape=jax.ShapeDtypeStruct((rows, cols), jnp.bfloat16),
-        in_specs=[pl.BlockSpec(memory_space=pl.ANY)] * 5,
+        in_specs=[pl.BlockSpec(memory_space=pltpu.HBM)] * 5,
         out_specs=pl.BlockSpec(memory_space=pltpu.VMEM),
         scratch_shapes=[
             *(pltpu.SMEM(x.shape, x.dtype) for x in operands[:3]),
@@ -317,7 +319,7 @@
             dma((n_c,)), dma((n_c,)),
         ],
         compiler_params=pltpu.CompilerParams(
-            collective_id=0, has_side_effects=True, vmem_limit_bytes=56 * 2**20
+            collective_id=0, has_side_effects=True, vmem_limit_bytes=held + 6 * 2**20
         ),
     )(*operands)
     factor = jnp.float32(wide * n_c)

time: 63.4 us -> 65.2 us (1.028)
  local copies, waits for them, and re-layouts: 0 us -> 4.1 us
  other arithmetic: 2.39 us -> 1.18 us
  Pallas kernels: 60.8 us -> 59.6 us
    unnamed x0 -> x10, local copies, waits for them, and re-layouts: none -> 4.1 us
    convert_element_type x1, other arithmetic: 2.39 us -> 1.18 us  [shards(): return (factor * density.astype(jnp.float32)).astype(jnp.bfloat16)]
    pallas_call x1, Pallas kernels: 60.8 us -> 59.6 us  [shards(): pl.pallas_call(functools.partial(kernel, n_r, n_c, n_p, nch), out_shape=j...]
where the time goes in v7:
time: 65.2 us; the launch traced here: 64.9 us
  Pallas kernels  59.6 us (91%)
  local copies, waits for them, and re-layouts  4.1 us (6%)
  other arithmetic  1.18 us (2%)
    pallas_call x1, Pallas kernels, shards(): pl.pallas_call(functools.partial(kernel, n_r, n_c, n_p, nch), out_shape=j...  59.6 us
    unnamed x10, local copies, waits for them, and re-layouts  4.1 us

profile of v7, /device:TPU:1, one launch (start us, length us, event | category | flops | bytes accessed | tf_op | source)
XLA Modules:
  0.0 64.9 jit_solution(196461740782207885)
XLA Ops:
  0.0 0.0 copy-start
  0.0 1.0 %copy-done = bf16[1,1024,256]{2,1,0:T(8,128)(2,1)S(1)} copy-done((bf16[1,1024,256]{2,1,0:T(8,128)(2,1)S(1)}, bf16[1,1024,256]{2,1,0:T(8,128)(2,1)}, u32[]{:S(2)}) %copy-start) | copy-done | bytes 524312
  1.0 0.0 copy-start.1
  1.0 1.0 %copy-done.1 = bf16[1,128,2048]{2,1,0:T(8,128)(2,1)S(1)} copy-done((bf16[1,128,2048]{2,1,0:T(8,128)(2,1)S(1)}, bf16[1,128,2048]{2,1,0:T(8,128)(2,1)}, u32[]{:S(2)}) %copy-start.1) | copy-done | bytes 524312
  2.1 0.0 copy-start.2
  2.1 0.7 %copy-done.2 = s32[8,4]{0,1:T(4,128)S(1)} copy-done((s32[8,4]{0,1:T(4,128)S(1)}, s32[8,4]{0,1:T(4,128)}, u32[]{:S(2)}) %copy-start.2) | copy-done | bytes 152
  2.8 0.0 copy-start.3
  2.8 0.7 %copy-done.3 = s32[1,8,2]{1,2,0:T(2,128)S(1)} copy-done((s32[1,8,2]{1,2,0:T(2,128)S(1)}, s32[1,8,2]{1,2,0:T(2,128)}, u32[]{:S(2)}) %copy-start.3) | copy-done | bytes 88
  3.4 0.0 copy-start.4
  3.4 0.7 %copy-done.4 = s32[1,1,16]{2,1,0:T(1,128)S(1)} copy-done((s32[1,1,16]{2,1,0:T(1,128)S(1)}, s32[1,1,16]{2,1,0:T(1,128)}, u32[]{:S(2)}) %copy-start.4) | copy-done | bytes 88
  4.1 59.6 %shard_map.55 = bf16[1024,512]{1,0:T(8,128)(2,1)S(1)} custom-call(s32[2,8]{1,0:T(2,128)S(1)} %bitcast.10, s32[1,16]{1,0:T(1,128)S(1)} %bitcast.11, s32[4,8]{1,0:T(4,128)S(1)} %bitcast.9, bf16[1024,256]{1,0:T(8,128)(2,1)S(1)} %bitcast.7, bf16[128,2048]{1,0:T(8,128)(2,1)S(1)} %bitcast.8), custom_call_target="tpu_custom_call" | custom-call | tf_op jit(solution)/shard_map/pallas_call | solution.py:298
  63.7 1.2 %multiply_convert_fusion = bf16[1024,512]{1,0:T(8,128)(2,1)} fusion(bf16[1024,512]{1,0:T(8,128)(2,1)S(1)} %shard_map.55), kind=kLoop, calls=%fused_computation | loop fusion | flops 1572864 | bytes 2097152 | tf_op jit(solution)/shard_map/convert_element_type | solution.py:326
Async XLA Ops:
  0.0 1.0 %copy-start = (bf16[1,1024,256]{2,1,0:T(8,128)(2,1)S(1)}, bf16[1,1024,256]{2,1,0:T(8,128)(2,1)}, u32[]{:S(2)}) copy-start(bf16[1,1024,256]{2,1,0:T(8,128)(2,1)} %param.5) | copy-start | bytes 1572868
  1.0 1.0 %copy-start.1 = (bf16[1,128,2048]{2,1,0:T(8,128)(2,1)S(1)}, bf16[1,128,2048]{2,1,0:T(8,128)(2,1)}, u32[]{:S(2)}) copy-start(bf16[1,128,2048]{2,1,0:T(8,128)(2,1)} %param.7) | copy-start | bytes 1572868
  2.1 0.7 %copy-start.2 = (s32[8,4]{0,1:T(4,128)S(1)}, s32[8,4]{0,1:T(4,128)}, u32[]{:S(2)}) copy-start(s32[8,4]{0,1:T(4,128)} %param.9) | copy-start | bytes 388
  2.8 0.7 %copy-start.3 = (s32[1,8,2]{1,2,0:T(2,128)S(1)}, s32[1,8,2]{1,2,0:T(2,128)}, u32[]{:S(2)}) copy-start(s32[1,8,2]{1,2,0:T(2,128)} %param.6) | copy-start | bytes 196
  3.4 0.7 %copy-start.4 = (s32[1,1,16]{2,1,0:T(1,128)S(1)}, s32[1,1,16]{2,1,0:T(1,128)}, u32[]{:S(2)}) copy-start(s32[1,1,16]{2,1,0:T(1,128)} %param.8) | copy-start | bytes 196

commit v8 on v6

--- a/solution.py
+++ b/solution.py
@@ -138,9 +138,11 @@
     )
     others(c, n_c, lambda cc: deg_copy(cc).start())
 
-    @pl.loop(0, nch)
-    def _(ch):
-        forward(p, ch)
+    @pl.when(is_end if turns else p >= 0)
+    def _():
+        @pl.loop(0, nch)
+        def _(ch):
+            forward(p, ch)
 
     def add_deg(cc):
         arrived(degr.at[cc], dr.at[cc])
@@ -241,6 +243,11 @@
             if d == 1:
                 if turns:
                     turn(ch)
+
+                    @pl.when(~is_end)
+                    def _():
+                        forward(p, ch)
+
                 own(0, ch)
             if d == 2:
                 own(1, ch)

time: 63.4 us -> 63.4 us (level)
  no operation moved by 1% of the time
where the time goes in v8:
time: 63.4 us; the launch traced here: 63.2 us
  Pallas kernels  60.8 us (96%)
  other arithmetic  2.39 us (4%)
    pallas_call x1, Pallas kernels, shards(): pl.pallas_call(functools.partial(kernel, n_r, n_c, n_p, nch), out_shape=j...  60.8 us
    convert_element_type x1, other arithmetic, shards(): return (factor * density.astype(jnp.float32)).astype(jnp.bfloat16)  2.39 us

profile of v8, /device:TPU:1, one launch (start us, length us, event | category | flops | bytes accessed | tf_op | source)
XLA Modules:
  0.0 63.2 jit_solution(16520025932657004615)
XLA Ops:
  0.0 60.8 %shard_map.55 = bf16[1024,512]{1,0:T(8,128)(2,1)} custom-call(s32[2,8]{1,0:T(2,128)} %bitcast.10, s32[1,16]{1,0:T(1,128)} %bitcast.11, s32[4,8]{1,0:T(4,128)} %bitcast.9, bf16[1024,256]{1,0:T(8,128)(2,1)} %bitcast.7, bf16[128,2048]{1,0:T(8,128)(2,1)} %bitcast.8), custom_call_target="tpu_custom_call" | custom-call | tf_op jit(solution)/shard_map/pallas_call | solution.py:303
  60.8 2.4 %multiply_convert_fusion = bf16[1024,512]{1,0:T(8,128)(2,1)} fusion(bf16[1024,512]{1,0:T(8,128)(2,1)} %shard_map.55), kind=kLoop, calls=%fused_computation | loop fusion | flops 1572864 | bytes 2097152 | tf_op jit(solution)/shard_map/convert_element_type | solution.py:331
